TPU v7x, 256 devices: a whole 4x4x8 slice. The times are simulated.
256 devices in a mesh: azi: 64 (over x, y_hi, z), axial: 4 (over y_lo, core).
Axes of the slice: x: 4, y: 4 (y_hi: 2, y_lo: 2; y = y_hi * 2 + y_lo), z: 8, core: 2. Of those that a mesh axis runs over, the one named last changes fastest.
Arguments:
- source_terms: float32 [3, 32, 64, 8192], P(None, 'axial', None, 'azi'), may hold values from -6 to 6
- diffusion: float32 [3, 32, 64, 8192], P(None, 'axial', None, 'azi'), may hold values from 0.5 to 5
- mass_coefficient: float32 [32, 64, 8192], P('axial', None, 'azi'), may hold values from 5 to 50
Outputs:
- solution: float32 [3, 32, 64, 8192], P(None, 'axial', None, 'azi')
- residual: float32 [3, 32, 64, 8192], P(None, 'axial', None, 'azi')
All inputs are finite; a program needn't handle non-finite values.
Results may differ from a plain program's by a relative error of at most 0.015.
Values sent between devices are 32-bit elements; how exact they have to be, the bound alone decides.
A program may use at most 64 MiB of HBM per device.

v0:
```python
import jax
import jax.numpy as jnp
import numpy as np
from jax import lax
from jax.sharding import PartitionSpec as P

ITERS = 2


def with_halo(value, sides, width):
    for axis, dim in sides:
        devices, length = (lax.axis_size(axis), value.shape[dim])
        up = [(i, (i + 1) % devices) for i in range(devices)]
        down = [(j, i) for i, j in up]
        last = lax.slice_in_dim(value, length - width, length, axis=dim)
        leading = lax.slice_in_dim(value, 0, width, axis=dim)
        before = lax.ppermute(last, axis, up)
        after = lax.ppermute(leading, axis, down)
        value = jnp.concatenate([before, value, after], axis=dim)
    return value


def gll_tables():
    degree = 7
    points = np.array(
        [
            -1.0,
            -0.8717401485096066,
            -0.5917001814331423,
            -0.2092992179024789,
            0.2092992179024789,
            0.5917001814331423,
            0.8717401485096066,
            1.0,
        ]
    )
    previous = np.ones(degree + 1)
    current = points.copy()
    for order in range(1, degree):
        following = ((2 * order + 1) * points * current - order * previous) / (order + 1)
        previous = current
        current = following
    weights = 2.0 / (degree * (degree + 1) * current * current)
    derivative = np.zeros((degree + 1, degree + 1))
    for first_index in range(degree + 1):
        for second_index in range(degree + 1):
            if first_index != second_index:
                derivative[first_index, second_index] = current[first_index] / (
                    current[second_index] * (points[first_index] - points[second_index])
                )
    derivative[0, 0] = -degree * (degree + 1) / 4.0
    derivative[degree, degree] = degree * (degree + 1) / 4.0
    return (weights, derivative)


def edge_masks(length, dimension):
    positions = jnp.arange(length) % 8
    shape_list = [1, 1, 1, 1]
    shape_list[dimension] = length
    starts = (positions == 0).astype(jnp.float32).reshape(shape_list)
    finish = (positions == 7).astype(jnp.float32).reshape(shape_list)
    return (starts, finish)


def join_edges(values, before, after, dimension):
    starts, finish = edge_masks(values.shape[dimension], dimension)
    return values + starts * before + finish * after


def join_radial(values):
    padded = jnp.pad(values, ((0, 0), (0, 0), (1, 1), (0, 0)))
    return join_edges(values, padded[:, :, :-2], padded[:, :, 2:], 2)


def assemble(local_terms):
    extended = with_halo(local_terms, (("azi", 3), ("axial", 1)), 1)
    index = lax.axis_index("axial")
    count = lax.axis_size("axial")
    rows = extended.shape[1]
    row_ids = jnp.arange(rows).reshape(1, rows, 1, 1)
    low_keep = (index > 0).astype(jnp.float32)
    high_keep = (index < count - 1).astype(jnp.float32)
    keeping = jnp.where(row_ids == 0, low_keep, jnp.where(row_ids == rows - 1, high_keep, 1.0))
    extended = extended * keeping
    along_azi = join_edges(extended[..., 1:-1], extended[..., :-2], extended[..., 2:], 3)
    along_axial = join_edges(along_azi[:, 1:-1], along_azi[:, :-2], along_azi[:, 2:], 1)
    return join_radial(along_axial)


def squares(residual, inverse_mult):
    return lax.psum(jnp.sum(residual * residual * inverse_mult, axis=(1, 2, 3)), ("azi", "axial"))


def shards(source_terms, diffusion, mass_coefficient):
    high = lax.Precision.HIGHEST
    weights, derivative = gll_tables()
    axial_len = source_terms.shape[1]
    radial_len = source_terms.shape[2]
    azimuth_len = source_terms.shape[3]
    matrix_z = jnp.asarray(np.kron(np.eye(axial_len // 8), derivative), jnp.float32)
    matrix_r = jnp.asarray(np.kron(np.eye(radial_len // 8), derivative), jnp.float32)
    matrix_a = jnp.asarray(np.kron(np.eye(azimuth_len // 8), derivative), jnp.float32)
    weight_z = np.tile(weights, axial_len // 8).reshape(axial_len, 1, 1)
    weight_r = np.tile(weights, radial_len // 8).reshape(1, radial_len, 1)
    weight_a = np.tile(weights, azimuth_len // 8).reshape(1, 1, azimuth_len)
    quadrature = jnp.asarray(weight_z * weight_r * weight_a, jnp.float32)
    scaled = quadrature[None] * diffusion
    massive = (quadrature * mass_coefficient)[None]
    index = lax.axis_index("axial")
    count = lax.axis_size("axial")
    local_rows = jnp.arange(axial_len)
    global_rows = index * axial_len + local_rows
    shared_z = (
        ((local_rows % 8 == 0) | (local_rows % 8 == 7))
        & (global_rows != 0)
        & (global_rows != count * axial_len - 1)
    )
    radial_rows = jnp.arange(radial_len)
    shared_r = (
        ((radial_rows % 8 == 0) | (radial_rows % 8 == 7))
        & (radial_rows != 0)
        & (radial_rows != radial_len - 1)
    )
    azimuth_rows = jnp.arange(azimuth_len)
    shared_a = (azimuth_rows % 8 == 0) | (azimuth_rows % 8 == 7)
    mult_total = (
        (1.0 + shared_z.astype(jnp.float32)).reshape(axial_len, 1, 1)
        * (1.0 + shared_r.astype(jnp.float32)).reshape(1, radial_len, 1)
        * (1.0 + shared_a.astype(jnp.float32)).reshape(1, 1, azimuth_len)
    )
    inverse_mult = (1.0 / mult_total)[None]

    def widen(scalars):
        return scalars[:, None, None, None]

    residual = assemble(source_terms)
    solution = jnp.zeros_like(residual)
    direction = residual
    norm_now = squares(residual, inverse_mult)
    for iteration in range(ITERS):
        grad_z = jnp.einsum("yz,fzra->fyra", matrix_z, direction, precision=high)
        grad_r = jnp.einsum("sr,fzra->fzsa", matrix_r, direction, precision=high)
        grad_a = jnp.einsum("ba,fzra->fzrb", matrix_a, direction, precision=high)
        total = massive * direction
        total = total + jnp.einsum("zy,fzra->fyra", matrix_z, scaled * grad_z, precision=high)
        total = total + jnp.einsum("rs,fzra->fzsa", matrix_r, scaled * grad_r, precision=high)
        total = total + jnp.einsum("ab,fzra->fzrb", matrix_a, scaled * grad_a, precision=high)
        applied = assemble(total)
        bending = lax.psum(
            jnp.sum(direction * applied * inverse_mult, axis=(1, 2, 3)), ("azi", "axial")
        )
        step_length = norm_now / bending
        solution = solution + widen(step_length) * direction
        residual = residual - widen(step_length) * applied
        if iteration + 1 < ITERS:
            norm_next = squares(residual, inverse_mult)
            direction = residual + widen(norm_next / norm_now) * direction
            norm_now = norm_next
    return (solution, residual)


def solution(mesh):
    in_specs = (
        P(None, "axial", None, "azi"),
        P(None, "axial", None, "azi"),
        P("axial", None, "azi"),
    )
    out_specs = (P(None, "axial", None, "azi"), P(None, "axial", None, "azi"))
    return jax.shard_map(shards, mesh=mesh, in_specs=in_specs, out_specs=out_specs, check_vma=False)
```

profile of v0, /device:TPU:1, one launch (start us, length us, event | category | flops | bytes accessed | tf_op | source)
XLA Modules:
  0.0 336.8 jit_solution(1156111485559056586)
XLA Ops:
  0.7 1.8 fusion.31
  2.8 11.3 %collective-permute-start.1 = (f32[3,8,64,1]{2,1,3,0:T(8,128)S(1)}, f32[3,8,64,1]{2,1,3,0:T(8,128)S(1)}, u32[]{:S(2)}, u32[]{:S(2)}) collective-permute-start(f32[3,8,64,1]{2,1,3,0:T(8,128)S(1)} %copy.55), channel_id=1, source_target_pairs={{4,0},{8,4},{12,8},{16,12},{20,16},{24,20},{28,24},{32,28},{36,32}... | collective-permute-start | bytes 18440 | tf_op jit(solution)/shard_map/ppermute | solution.py:18
  14.6 0.5 copy.24
  15.3 7.4 %collective-permute-done = f32[3,8,64,1]{2,1,3,0:T(8,128)S(1)} collective-permute-done((f32[3,8,64,1]{2,1,3,0:T(8,128)S(1)}, f32[3,8,64,1]{2,1,3,0:T(8,128)S(1)}, u32[]{:S(2)}, u32[]{:S(2)}) %collective-permute-start) | collective-permute-done | bytes 6176 | tf_op jit(solution)/shard_map/ppermute | solution.py:17
  22.7 0.4 copy.23
  23.0 0.4 copy.25
  23.4 1.3 pad_maximum_fusion.8
  24.7 2.6 collective-permute-start.2
  27.2 0.5 collective-permute-start.3
  27.8 2.1 collective-permute-done.2
  29.9 3.5 %collective-permute-done.3 = f32[3,1,64,130]{3,1,2,0:T(1,128)S(1)} collective-permute-done((f32[3,1,64,130]{3,1,2,0:T(1,128)S(1)}, f32[3,1,64,130]{3,1,2,0:T(1,128)S(1)}, u32[]{:S(2)}, u32[]{:S(2)}) %collective-permute-start.3) | collective-permute-done | bytes 99872 | tf_op jit(solution)/shard_map/ppermute | solution.py:18
  33.4 1.5 maximum_multiply_fusion
  34.9 0.9 fusion.4
  36.3 0.6 copy-done
  36.9 0.9 fusion.8
  37.9 0.8 fusion.33
  38.7 0.8 fusion.32
  39.8 0.8 convolution_multiply_fusion.1
  40.6 1.7 fusion.10
  42.3 1.1 convolution_add_fusion.1
  43.4 1.2 fusion.30
  44.6 2.0 copy.30
  46.6 0.9 copy.31
  47.5 1.6 collective-permute-start.4
  49.1 0.6 fusion.26
  49.7 6.5 %collective-permute-done.4 = f32[3,8,64,1]{2,1,3,0:T(8,128)} collective-permute-done((f32[3,8,64,1]{2,1,3,0:T(8,128)}, f32[3,8,64,1]{2,1,3,0:T(8,128)}, u32[]{:S(2)}, u32[]{:S(2)}) %collective-permute-start.4) | collective-permute-done | bytes 6176 | tf_op jit(solution)/shard_map/ppermute | solution.py:17
  56.2 1.0 copy.32
  57.3 1.9 copy.33
  59.2 2.7 pad_maximum_fusion.5
  62.0 1.1 collective-permute-start.6
  63.1 0.8 multiply_divide_fusion
  63.9 2.6 collective-permute-done.6
  66.5 2.4 collective-permute-done.7
  68.9 2.2 maximum_multiply_fusion.1
  71.1 0.9 fusion.2
  72.3 0.5 multiply_reduce_fusion.2
  72.8 72.2 %all-reduce.3 = (f32[3]{0:T(128)S(1)}, f32[3]{0:T(128)S(1)}) all-reduce(f32[3]{0:T(128)S(1)} %get-tuple-element.7, f32[3]{0:T(128)S(1)} %get-tuple-element.6), channel_id=1, replica_groups=mesh['azi'=64,'axial'=4] {'azi','axial'}, use_global_device_ids=true, to_apply=%region_1.2 | all-reduce | flops 6 | bytes 48 | tf_op jit(solution)/shard_map/psum | solution.py:91
  144.9 1.4 multiply_reduce_fusion.1
  146.3 73.7 %psum.30 = f32[3]{0:T(128)S(1)} all-reduce(f32[3]{0:T(128)S(1)} %multiply_reduce_fusion.1), channel_id=1, replica_groups=mesh['azi'=64,'axial'=4] {'azi','axial'}, use_global_device_ids=true, to_apply=%region_5.6 | all-reduce | flops 3 | bytes 24 | tf_op jit(solution)/shard_map/psum | solution.py:91
  220.3 0.8 convolution_multiply_fusion
  221.1 0.9 fusion.6
  222.1 0.8 fusion.34
  222.9 0.8 fusion.35
  224.0 1.7 fusion.11
  225.7 1.1 convolution_add_fusion
  226.8 1.4 fusion.29
  228.2 1.4 copy.37
  229.6 1.0 collective-permute-start.8
  230.6 1.4 copy.38
  232.0 6.3 %collective-permute-start.9 = (f32[3,8,64,1]{2,1,3,0:T(8,128)S(1)}, f32[3,8,64,1]{2,1,3,0:T(8,128)S(1)}, u32[]{:S(2)}, u32[]{:S(2)}) collective-permute-start(f32[3,8,64,1]{2,1,3,0:T(8,128)S(1)} %copy.38), channel_id=1, source_target_pairs={{4,0},{8,4},{12,8},{16,12},{20,16},{24,20},{28,24},{32,28},{36,32}... | collective-permute-start | bytes 18440 | tf_op jit(solution)/shard_map/ppermute | solution.py:18
  238.3 1.2 copy.39
  239.5 1.2 copy.40
  240.7 3.3 pad_maximum_fusion.2
  244.1 2.2 collective-permute-start.10
  246.6 2.9 collective-permute-done.10
  249.4 2.6 collective-permute-done.11
  252.1 1.5 maximum_multiply_fusion.2
  253.6 0.9 fusion
  254.7 0.7 copy-done.7
  255.4 0.4 multiply_reduce_fusion
  255.8 78.3 %psum.31 = f32[3]{0:T(128)S(1)} all-reduce(f32[3]{0:T(128)S(1)} %get-tuple-element.10), channel_id=1, replica_groups=mesh['azi'=64,'axial'=4] {'azi','axial'}, use_global_device_ids=true, to_apply=%region_7.8 | all-reduce | flops 3 | bytes 24 | tf_op jit(solution)/shard_map/psum | solution.py:149
  334.1 0.4 multiply_subtract_fusion
  334.5 1.0 copy.42
  335.5 1.0 copy.41
  (75 shorter events, 3.0 us)
Async XLA Ops:
  0.6 14.4 %copy-start.1 = (f32[8,64,128]{2,1,0:T(8,128)S(1)}, f32[8,64,128]{2,1,0:T(8,128)}, u32[]{:S(2)}) copy-start(f32[8,64,128]{2,1,0:T(8,128)} %constant.119.clone) | copy-start | bytes 786436
  0.6 13.9 %copy-start.2 = (f32[3,8,64,128]{3,2,1,0:T(8,128)S(1)}, f32[3,8,64,128]{3,2,1,0:T(8,128)}, u32[]{:S(2)}) copy-start(f32[3,8,64,128]{3,2,1,0:T(8,128)} %param.7) | copy-start | bytes 2359300
  0.7 14.4 %copy-start.12 = (f32[8,64,128]{2,1,0:T(8,128)S(1)}, f32[8,64,128]{2,1,0:T(8,128)}, u32[]{:S(2)}) copy-start(f32[8,64,128]{2,1,0:T(8,128)} %param.9) | copy-start | bytes 786436
  2.8 20.3 %collective-permute-start.1 = (f32[3,8,64,1]{2,1,3,0:T(8,128)S(1)}, f32[3,8,64,1]{2,1,3,0:T(8,128)S(1)}, u32[]{:S(2)}, u32[]{:S(2)}) collective-permute-start(f32[3,8,64,1]{2,1,3,0:T(8,128)S(1)} %copy.55), channel_id=1, source_target_pairs={{4,0},{8,4},{12,8},{16,12},{20,16},{24,20},{28,24},{32,28},{36,32}... | collective-permute-start | bytes 18440 | tf_op jit(solution)/shard_map/ppermute | solution.py:18
  14.3 8.3 %collective-permute-start = (f32[3,8,64,1]{2,1,3,0:T(8,128)S(1)}, f32[3,8,64,1]{2,1,3,0:T(8,128)S(1)}, u32[]{:S(2)}, u32[]{:S(2)}) collective-permute-start(f32[3,8,64,1]{2,1,3,0:T(8,128)S(1)} %copy.54), channel_id=1, source_target_pairs={{0,4},{4,8},{8,12},{12,16},{16,20},{20,24},{24,28},{28,32},{32,36}... | collective-permute-start | bytes 18440 | tf_op jit(solution)/shard_map/ppermute | solution.py:17
  14.4 20.5 %copy-start.18 = (f32[128]{0:T(128)}, f32[128]{0:T(128)S(1)}, u32[]{:S(2)}) copy-start(f32[128]{0:T(128)S(1)} %get-tuple-element.27) | copy-start | bytes 1540
  14.4 20.4 %copy-start.21 = (f32[128]{0:T(128)}, f32[128]{0:T(128)S(1)}, u32[]{:S(2)}) copy-start(f32[128]{0:T(128)S(1)} %get-tuple-element.28) | copy-start | bytes 1540
  14.5 21.4 %copy-start.14 = (f32[8]{0:T(128)}, f32[8]{0:T(128)S(1)}, u32[]{:S(2)}) copy-start(f32[8]{0:T(128)S(1)} %get-tuple-element.30) | copy-start | bytes 100
  15.3 25.3 %copy-start.8 = (f32[8,64,128]{2,0,1:T(8,128)}, f32[8,64,128]{2,0,1:T(8,128)S(1)}, u32[]{:S(2)}) copy-start(f32[8,64,128]{2,0,1:T(8,128)S(1)} %copy.26) | copy-start | bytes 786436
  24.7 5.2 %collective-permute-start.2 = (f32[3,1,64,130]{3,1,2,0:T(1,128)S(1)}, f32[3,1,64,130]{3,1,2,0:T(1,128)S(1)}, u32[]{:S(2)}, u32[]{:S(2)}) collective-permute-start(f32[3,1,64,130]{3,1,2,0:T(1,128)S(1)} %get-tuple-element.17), channel_id=1, source_target_pairs={{0,1},{1,2},{2,3},{3,0},{4,5},{5,6},{6,7},{7,4},{8,9},{9,10},{10,1... | collective-permute-start | bytes 299528 | tf_op jit(solution)/shard_map/ppermute | solution.py:17
  27.2 6.1 %collective-permute-start.3 = (f32[3,1,64,130]{3,1,2,0:T(1,128)S(1)}, f32[3,1,64,130]{3,1,2,0:T(1,128)S(1)}, u32[]{:S(2)}, u32[]{:S(2)}) collective-permute-start(f32[3,1,64,130]{3,1,2,0:T(1,128)S(1)} %get-tuple-element.18), channel_id=1, source_target_pairs={{1,0},{2,1},{3,2},{0,3},{5,4},{6,5},{7,6},{4,7},{9,8},{10,9},{11,1... | collective-permute-start | bytes 299528 | tf_op jit(solution)/shard_map/ppermute | solution.py:18
  27.8 8.0 %copy-start.16 = (f32[10]{0:T(128)}, f32[10]{0:T(128)S(1)}, u32[]{:S(2)}) copy-start(f32[10]{0:T(128)S(1)} %compare_select_fusion.1) | copy-start | bytes 124
  35.8 1.1 copy-start
  35.8 1.1 copy-start.11
  36.1 2.7 copy-start.13
  37.9 1.9 copy-start.10
  47.5 9.8 %collective-permute-start.5 = (f32[3,8,64,1]{2,1,3,0:T(8,128)}, f32[3,8,64,1]{2,1,3,0:T(8,128)}, u32[]{:S(2)}, u32[]{:S(2)}) collective-permute-start(f32[3,8,64,1]{2,1,3,0:T(8,128)} %copy.31), channel_id=1, source_target_pairs={{4,0},{8,4},{12,8},{16,12},{20,16},{24,20},{28,24},{32,28},{36,32}... | collective-permute-start | bytes 18440 | tf_op jit(solution)/shard_map/ppermute | solution.py:18
  47.5 8.7 %collective-permute-start.4 = (f32[3,8,64,1]{2,1,3,0:T(8,128)}, f32[3,8,64,1]{2,1,3,0:T(8,128)}, u32[]{:S(2)}, u32[]{:S(2)}) collective-permute-start(f32[3,8,64,1]{2,1,3,0:T(8,128)} %copy.30), channel_id=1, source_target_pairs={{0,4},{4,8},{8,12},{12,16},{16,20},{20,24},{24,28},{28,32},{32,36}... | collective-permute-start | bytes 18440 | tf_op jit(solution)/shard_map/ppermute | solution.py:17
  59.2 9.7 %copy-start.4 = (f32[3,8,64,1]{3,1,2,0:T(8,128)S(1)}, f32[3,8,64,1]{3,1,2,0:T(8,128)}, u32[]{:S(2)}) copy-start(f32[3,8,64,1]{3,1,2,0:T(8,128)} %copy.33) | copy-start | bytes 18436
  61.9 9.2 %copy-start.19 = (f32[128]{0:T(128)S(1)}, f32[128]{0:T(128)}, u32[]{:S(2)}) copy-start(f32[128]{0:T(128)} %copy-done.18) | copy-start | bytes 1540
  61.9 9.2 %copy-start.22 = (f32[128]{0:T(128)S(1)}, f32[128]{0:T(128)}, u32[]{:S(2)}) copy-start(f32[128]{0:T(128)} %copy-done.21) | copy-start | bytes 1540
  62.0 4.5 %collective-permute-start.6 = (f32[3,1,64,130]{3,1,2,0:T(1,128)S(1)}, f32[3,1,64,130]{3,1,2,0:T(1,128)S(1)}, u32[]{:S(2)}, u32[]{:S(2)}) collective-permute-start(f32[3,1,64,130]{3,1,2,0:T(1,128)S(1)} %get-tuple-element.15), channel_id=1, source_target_pairs={{0,1},{1,2},{2,3},{3,0},{4,5},{5,6},{6,7},{7,4},{8,9},{9,10},{10,1... | collective-permute-start | bytes 299528 | tf_op jit(solution)/shard_map/ppermute | solution.py:17
  63.1 5.9 %collective-permute-start.7 = (f32[3,1,64,130]{3,1,2,0:T(1,128)S(1)}, f32[3,1,64,130]{3,1,2,0:T(1,128)S(1)}, u32[]{:S(2)}, u32[]{:S(2)}) collective-permute-start(f32[3,1,64,130]{3,1,2,0:T(1,128)S(1)} %get-tuple-element.16), channel_id=1, source_target_pairs={{1,0},{2,1},{3,2},{0,3},{5,4},{6,5},{7,6},{4,7},{9,8},{10,9},{11,1... | collective-permute-start | bytes 299528 | tf_op jit(solution)/shard_map/ppermute | solution.py:18
  63.9 8.3 %copy-start.6 = (f32[8,64,128]{2,0,1:T(8,128)}, f32[8,64,128]{2,0,1:T(8,128)S(1)}, u32[]{:S(2)}) copy-start(f32[8,64,128]{2,0,1:T(8,128)S(1)} %multiply_divide_fusion) | copy-start | bytes 786436
  71.1 0.9 copy-start.15
  222.1 1.9 copy-start.9
  228.2 23.9 %copy-start.17 = (f32[10]{0:T(128)S(1)}, f32[10]{0:T(128)}, u32[]{:S(2)}) copy-start(f32[10]{0:T(128)} %copy-done.16) | copy-start | bytes 124
  229.6 8.7 %collective-permute-start.8 = (f32[3,8,64,1]{2,1,3,0:T(8,128)S(1)}, f32[3,8,64,1]{2,1,3,0:T(8,128)S(1)}, u32[]{:S(2)}, u32[]{:S(2)}) collective-permute-start(f32[3,8,64,1]{2,1,3,0:T(8,128)S(1)} %copy.37), channel_id=1, source_target_pairs={{0,4},{4,8},{8,12},{12,16},{16,20},{20,24},{24,28},{28,32},{32,36}... | collective-permute-start | bytes 18440 | tf_op jit(solution)/shard_map/ppermute | solution.py:17
  232.0 7.5 %collective-permute-start.9 = (f32[3,8,64,1]{2,1,3,0:T(8,128)S(1)}, f32[3,8,64,1]{2,1,3,0:T(8,128)S(1)}, u32[]{:S(2)}, u32[]{:S(2)}) collective-permute-start(f32[3,8,64,1]{2,1,3,0:T(8,128)S(1)} %copy.38), channel_id=1, source_target_pairs={{4,0},{8,4},{12,8},{16,12},{20,16},{24,20},{28,24},{32,28},{36,32}... | collective-permute-start | bytes 18440 | tf_op jit(solution)/shard_map/ppermute | solution.py:18
  240.7 11.3 %copy-start.3 = (f32[3,8,64,1]{3,1,2,0:T(8,128)S(1)}, f32[3,8,64,1]{3,1,2,0:T(8,128)}, u32[]{:S(2)}) copy-start(f32[3,8,64,1]{3,1,2,0:T(8,128)} %copy.39) | copy-start | bytes 18436
  240.7 11.3 %copy-start.5 = (f32[3,8,64,1]{3,1,2,0:T(8,128)S(1)}, f32[3,8,64,1]{3,1,2,0:T(8,128)}, u32[]{:S(2)}) copy-start(f32[3,8,64,1]{3,1,2,0:T(8,128)} %copy.40) | copy-start | bytes 18436
  244.0 9.6 %copy-start.20 = (f32[128]{0:T(128)S(1)}, f32[128]{0:T(128)}, u32[]{:S(2)}) copy-start(f32[128]{0:T(128)} %copy-done.18) | copy-start | bytes 1540
  244.0 9.6 %copy-start.23 = (f32[128]{0:T(128)S(1)}, f32[128]{0:T(128)}, u32[]{:S(2)}) copy-start(f32[128]{0:T(128)} %copy-done.21) | copy-start | bytes 1540
  244.1 5.4 %collective-permute-start.10 = (f32[3,1,64,130]{3,1,2,0:T(1,128)S(1)}, f32[3,1,64,130]{3,1,2,0:T(1,128)S(1)}, u32[]{:S(2)}, u32[]{:S(2)}) collective-permute-start(f32[3,1,64,130]{3,1,2,0:T(1,128)S(1)} %get-tuple-element.13), channel_id=1, source_target_pairs={{0,1},{1,2},{2,3},{3,0},{4,5},{5,6},{6,7},{7,4},{8,9},{9,10},{10,1... | collective-permute-start | bytes 299528 | tf_op jit(solution)/shard_map/ppermute | solution.py:17
  246.3 5.8 %collective-permute-start.11 = (f32[3,1,64,130]{3,1,2,0:T(1,128)S(1)}, f32[3,1,64,130]{3,1,2,0:T(1,128)S(1)}, u32[]{:S(2)}, u32[]{:S(2)}) collective-permute-start(f32[3,1,64,130]{3,1,2,0:T(1,128)S(1)} %get-tuple-element.14), channel_id=1, source_target_pairs={{1,0},{2,1},{3,2},{0,3},{5,4},{6,5},{7,6},{4,7},{9,8},{10,9},{11,1... | collective-permute-start | bytes 299528 | tf_op jit(solution)/shard_map/ppermute | solution.py:18
  254.5 1.0 copy-start.7
where the time goes:
time: 342 us; the launch traced here: 337 us
  blocking collectives  224 us (65%)
  waiting for transfers between devices  30 us (9%)
  starting transfers between devices  27 us (8%)
  other arithmetic  21 us (6%)
  local copies, waits for them, and re-layouts  20.8 us (6%)
  matrix products  12.3 us (4%)
    psum x2, blocking collectives, squares(): lax.psum(jnp.sum(residual * residual * inverse_mult, axis=(1, 2, 3)), ('a...  146 us
    psum x1, blocking collectives, shards(): lax.psum(jnp.sum(direction * applied * inverse_mult, axis=(1, 2, 3)), ('a...  78.3 us
    ppermute x6, waiting for transfers between devices, with_halo(): before = lax.ppermute(last, axis, up)  21.4 us
    ppermute x6, starting transfers between devices, with_halo(): after = lax.ppermute(leading, axis, down)  18.4 us
    ppermute x6, starting transfers between devices, with_halo(): before = lax.ppermute(last, axis, up)  8.6 us
    ppermute x6, waiting for transfers between devices, with_halo(): after = lax.ppermute(leading, axis, down)  8.56 us
    slice x5, local copies, waits for them, and re-layouts, with_halo(): last = lax.slice_in_dim(value, length - width, length, axis=dim)  7.77 us
    slice x3, other arithmetic, with_halo(): last = lax.slice_in_dim(value, length - width, length, axis=dim)  7.3 us
  transfers between devices with their start and end apart: 12, of which 8 were waited for; matrix products, arithmetic and copies ran while one was open for 2% of the time, Pallas kernels for 0%

commit v1 on v0

v1 whole, which is shorter than its diff:
```python
import jax
import jax.numpy as jnp
import numpy as np
from jax import lax
from jax.experimental import pallas as pl
from jax.experimental.pallas import tpu as pltpu
from jax.sharding import PartitionSpec as P

MESH = pl.DeviceIdType.MESH
FIELDS = 3
PHASES = 3
LANES = 128
TILES = 64


def gll_tables():
    degree = 7
    points = np.array(
        [
            -1.0,
            -0.8717401485096066,
            -0.5917001814331423,
            -0.2092992179024789,
            0.2092992179024789,
            0.5917001814331423,
            0.8717401485096066,
            1.0,
        ]
    )
    previous = np.ones(degree + 1)
    current = points.copy()
    for order in range(1, degree):
        following = ((2 * order + 1) * points * current - order * previous) / (order + 1)
        previous = current
        current = following
    weights = 2.0 / (degree * (degree + 1) * current * current)
    derivative = np.zeros((degree + 1, degree + 1))
    for first_index in range(degree + 1):
        for second_index in range(degree + 1):
            if first_index != second_index:
                derivative[first_index, second_index] = current[first_index] / (
                    current[second_index] * (points[first_index] - points[second_index])
                )
    derivative[0, 0] = -degree * (degree + 1) / 4.0
    derivative[degree, degree] = degree * (degree + 1) / 4.0
    return (weights, derivative)


WEIGHTS, DERIVATIVE = gll_tables()


def lane_operators():
    whole = np.kron(np.eye(LANES // 8), DERIVATIVE)
    return np.stack([whole.T, whole]).astype(np.float32)


def mix(matrix, values):
    even = [values[i] + values[7 - i] for i in range(4)]
    odd = [values[i] - values[7 - i] for i in range(4)]
    result = [None] * 8
    for j in range(4):
        from_even = None
        from_odd = None
        for i in range(4):
            a = float(0.5 * (matrix[j, i] + matrix[j, 7 - i])) * even[i]
            b = float(0.5 * (matrix[j, i] - matrix[j, 7 - i])) * odd[i]
            from_even = a if from_even is None else from_even + a
            from_odd = b if from_odd is None else from_odd + b
        result[j] = from_odd + from_even
        result[7 - j] = from_odd - from_even
    return result


def azi_shift(azi, axial, count):
    return lax.rem(azi + count + 64, 64), axial


def column_partner(azi, axial, index):
    z = lax.rem(azi, 8)
    other = azi - z + lax.rem(z + index // 2, 8)
    core = lax.rem(axial, 2)
    flipped = axial + (1 - 2 * core) if index % 2 else axial
    return other, flipped


def plane_partner(azi, axial, index):
    x = azi // 16
    y_hi = lax.rem(azi // 8, 2)
    z = lax.rem(azi, 8)
    x = lax.rem(x + index // 4, 4)
    y_hi = lax.rem(y_hi + (index // 2) % 2, 2)
    return x * 16 + y_hi * 8 + z, lax.rem(axial + 2 * (index % 2), 4)


def kernel(
    src_hbm,
    dif_hbm,
    mas_hbm,
    wts_hbm,
    sol,
    res,
    src,
    dif,
    mas,
    lane_ops,
    wts,
    scaled,
    massive,
    own,
    full,
    raw,
    packed,
    got_plane,
    got_packed,
    dots,
    ar_send,
    ar_got,
    in_sem,
    send_sem,
    recv_sem,
    ar_send_sem,
    ar_recv_sem,
):
    azi = lax.axis_index("azi")
    axial = lax.axis_index("axial")
    has_low = axial > 0
    has_high = axial < 3

    loads = []
    for f in range(FIELDS):
        loads.append(pltpu.make_async_copy(src_hbm.at[f], src.at[f], in_sem.at[f]))
    for f in range(FIELDS):
        loads.append(pltpu.make_async_copy(dif_hbm.at[f], dif.at[f], in_sem.at[3 + f]))
    loads.append(pltpu.make_async_copy(mas_hbm, mas, in_sem.at[6]))
    loads.append(pltpu.make_async_copy(wts_hbm, lane_ops, in_sem.at[7]))
    for copy in loads:
        copy.start()

    up = lax.rem(azi + 1, 64)
    down = lax.rem(azi + 63, 64)
    barrier = pltpu.get_barrier_semaphore()

    def greet(device):
        pl.semaphore_signal(barrier, inc=1, device_id=device, device_id_type=MESH)

    greet((up, axial))
    greet((down, axial))

    @pl.when(has_low)
    def _():
        for other in (up, azi, down):
            greet((other, axial - 1))

    @pl.when(has_high)
    def _():
        for other in (up, azi, down):
            greet((other, axial + 1))

    column = [column_partner(azi, axial, j) for j in range(1, 16)]
    plane = [plane_partner(azi, axial, j) for j in range(1, 16)]
    for device in column + plane:
        greet(device)

    @pl.when(jnp.logical_not(has_low))
    def _():
        for ph in range(PHASES):
            for f in range(FIELDS):
                got_plane[ph, f, 0] = jnp.zeros((8, 8, LANES), jnp.float32)
                got_packed[ph, f, 2] = jnp.zeros((8, LANES), jnp.float32)
                got_packed[ph, f, 3] = jnp.zeros((8, LANES), jnp.float32)

    @pl.when(jnp.logical_not(has_high))
    def _():
        for ph in range(PHASES):
            for f in range(FIELDS):
                got_plane[ph, f, 1] = jnp.zeros((8, 8, LANES), jnp.float32)
                got_packed[ph, f, 4] = jnp.zeros((8, LANES), jnp.float32)
                got_packed[ph, f, 5] = jnp.zeros((8, LANES), jnp.float32)

    lane = lax.broadcasted_iota(jnp.int32, (8, LANES), 1)
    sub = lax.broadcasted_iota(jnp.int32, (8, LANES), 0)
    in_element = lane % 8
    starts = (in_element == 0) & (lane != 0)
    finish = (in_element == 7) & (lane != LANES - 1)
    outer = (lane == 0) | (lane == LANES - 1)
    even_lane = lane % 2 == 0
    group_of_lane = ((lane + 1) % LANES) // 16
    pair_of_lane = ((lane + 1) % LANES) // 2
    zeros = jnp.zeros((8, LANES), jnp.float32)

    def join_lanes(tile):
        before = pltpu.roll(tile, 1, 1)
        after = pltpu.roll(tile, LANES - 1, 1)
        return tile + jnp.where(starts, before, jnp.where(finish, after, 0.0))

    def join_rows(tiles):
        first, last = tiles[0], tiles[7]
        tiles[0] = first + jnp.where(sub > 0, pltpu.roll(last, 1, 0), 0.0)
        tiles[7] = last + jnp.where(sub < 7, pltpu.roll(first, 7, 0), 0.0)
        return tiles

    def assemble_own(ph, f, z, tiles, faces):
        tiles = join_rows(list(tiles))
        line = zeros
        for i in range(8):
            tile = join_lanes(tiles[i])
            own[ph, f, z * 8 + i] = tile
            turned = pltpu.roll(tile, 2 * i, 1) if i else tile
            line = jnp.where(pair_of_lane == i, turned, line)
        return jnp.where(group_of_lane == z, pltpu.roll(line, z * 16, 1), faces)

    def copies(ph, f):
        def remote(source, target, slot, device):
            return pltpu.make_async_remote_copy(
                src_ref=source,
                dst_ref=target,
                send_sem=send_sem.at[ph, f, slot],
                recv_sem=recv_sem.at[ph, f, slot],
                device_id=device,
                device_id_type=MESH,
            )

        tile = packed.at[ph, f]
        slots = got_packed.at[ph, f]
        always = [
            remote(tile, slots.at[0], 0, (up, axial)),
            remote(tile, slots.at[1], 1, (down, axial)),
        ]
        above = [
            remote(tile, slots.at[2], 2, (up, axial + 1)),
            remote(tile, slots.at[3], 3, (down, axial + 1)),
            remote(own.at[ph, f, pl.ds(56, 8)], got_plane.at[ph, f, 0], 6, (azi, axial + 1)),
        ]
        below = [
            remote(tile, slots.at[4], 4, (up, axial - 1)),
            remote(tile, slots.at[5], 5, (down, axial - 1)),
            remote(own.at[ph, f, pl.ds(0, 8)], got_plane.at[ph, f, 1], 7, (azi, axial - 1)),
        ]
        return always, above, below

    def send(ph, f):
        always, above, below = copies(ph, f)
        for copy in always:
            copy.start()

        @pl.when(has_high)
        def _():
            for copy in above:
                copy.start()

        @pl.when(has_low)
        def _():
            for copy in below:
                copy.start()

    def receive(ph, f):
        always, above, below = copies(ph, f)
        for copy in always:
            copy.wait_recv()

        @pl.when(has_low)
        def _():
            for copy in above:
                copy.wait_recv()

        @pl.when(has_high)
        def _():
            for copy in below:
                copy.wait_recv()

    def finish_sends(ph, f):
        always, above, below = copies(ph, f)
        for copy in always:
            copy.wait_send()

        @pl.when(has_high)
        def _():
            for copy in above:
                copy.wait_send()

        @pl.when(has_low)
        def _():
            for copy in below:
                copy.wait_send()

    def complete(ph, f, use, carry):
        receive(ph, f)

        def faced(left, right):
            return jnp.where(
                even_lane, pltpu.roll(left, 1, 1), pltpu.roll(right, LANES - 1, 1)
            )

        slots = [got_packed[ph, f, s] for s in range(6)]
        faces = faced(slots[0], slots[1])
        low = pltpu.roll(faced(slots[2], slots[3]), LANES - 112, 1)
        high = pltpu.roll(faced(slots[4], slots[5]), 112, 1)
        faces = faces + jnp.where(group_of_lane == 0, low, 0.0)
        faces = faces + jnp.where(group_of_lane == 7, high, 0.0)

        def one(z, carry, plane):
            line = pltpu.roll(faces, lax.rem(LANES - z * 16, LANES), 1)
            for i in range(8):
                turned = pltpu.roll(line, LANES - 2 * i, 1) if i else line
                tile = own[ph, f, z * 8 + i] + jnp.where(outer, turned, 0.0)
                if plane is not None:
                    tile = tile + got_plane[ph, f, plane, i]
                carry = use(z, i, tile, carry)
            return carry

        carry = one(0, carry, 0)
        carry = lax.fori_loop(1, 7, lambda z, c: one(z, c, None), carry)
        return one(7, carry, 1)

    def split_dot(values, which):
        high = values.astype(jnp.bfloat16)
        low = (values - high.astype(jnp.float32)).astype(jnp.bfloat16)
        both = jnp.dot(
            jnp.concatenate([high, low], axis=1), wts[which], preferred_element_type=jnp.float32
        )
        return both[:, :LANES] + both[:, LANES:]

    def operate(k, f):
        values = full[k, f].reshape(TILES * 8, LANES)
        gradient = split_dot(values, 0) * scaled[f].reshape(TILES * 8, LANES)
        raw[f] = split_dot(gradient, 1).reshape(TILES, 8, LANES)

        def along_axial(i, carry):
            tiles = [full[k, f, z * 8 + i] for z in range(8)]
            gradient = mix(DERIVATIVE, tiles)
            gradient = [scaled[f, z * 8 + i] * gradient[z] for z in range(8)]
            back = mix(DERIVATIVE.T, gradient)
            for z in range(8):
                raw[f, z * 8 + i] = raw[f, z * 8 + i] + (back[z] + massive[z * 8 + i] * tiles[z])
            return carry

        lax.fori_loop(0, 8, along_axial, 0)

        def along_radius(z, carry):
            total, faces = carry
            tiles = [full[k, f, z * 8 + i] for i in range(8)]
            gradient = mix(DERIVATIVE, tiles)
            gradient = [scaled[f, z * 8 + i] * gradient[i] for i in range(8)]
            back = mix(DERIVATIVE.T, gradient)
            back = [raw[f, z * 8 + i] + back[i] for i in range(8)]
            for i in range(8):
                total = total + tiles[i] * back[i]
                raw[f, z * 8 + i] = back[i]
            return total, assemble_own(k + 1, f, z, back, faces)

        total, faces = lax.fori_loop(0, 8, along_radius, (zeros, zeros))
        packed[k + 1, f] = faces
        return total

    def native(ref, f, z, i):
        return ref[f, z, pl.ds(i, 8, stride=8), :]

    for f in range(FIELDS):
        loads[f].wait()

        def gather(z, faces):
            return assemble_own(0, f, z, [native(src, f, z, i) for i in range(8)], faces)

        packed[0, f] = lax.fori_loop(0, 8, gather, zeros)

    around = axial * 0 + 2 + 30 + jnp.where(has_low, 3, 0) + jnp.where(has_high, 3, 0)
    pl.semaphore_wait(barrier, around)
    for f in range(FIELDS):
        send(0, f)

    weight_a = jnp.zeros((8, LANES), jnp.float32)
    for i in range(8):
        weight_a = jnp.where(in_element == i, float(WEIGHTS[i]), weight_a)
    loads[6].wait()
    for f in range(FIELDS):
        loads[3 + f].wait()
    loads[7].wait()
    for which in range(2):
        high = lane_ops[which].astype(jnp.bfloat16)
        low = (lane_ops[which] - high.astype(jnp.float32)).astype(jnp.bfloat16)
        wts[which, :LANES, :LANES] = high
        wts[which, :LANES, LANES:] = low
        wts[which, LANES:, :LANES] = high
        wts[which, LANES:, LANES:] = jnp.zeros((LANES, LANES), jnp.bfloat16)
    for z in range(8):
        for i in range(8):
            weight = float(WEIGHTS[z] * WEIGHTS[i]) * weight_a
            massive[z * 8 + i] = weight * mas[z, pl.ds(i, 8, stride=8), :]
            for f in range(FIELDS):
                scaled[f, z * 8 + i] = weight * native(dif, f, z, i)

    for f in range(FIELDS):

        def keep_rhs(z, i, tile, total):
            full[0, f, z * 8 + i] = tile
            return total + tile * native(src, f, z, i)

        dots[f] = complete(0, f, keep_rhs, zeros)
        dots[3 + f] = operate(0, f)
        send(1, f)

    for f in range(FIELDS):

        def keep_image(z, i, tile, total):
            full[1, f, z * 8 + i] = tile
            return total + tile * raw[f, z * 8 + i]

        dots[6 + f] = complete(1, f, keep_image, zeros)
        dots[9 + f] = operate(1, f)
        send(2, f)

    lane_row = lax.broadcasted_iota(jnp.int32, (1, LANES), 1)
    row = jnp.zeros((1, LANES), jnp.float32)
    for j in range(12):
        part = jnp.sum(jnp.sum(dots[j], axis=0, keepdims=True), axis=1, keepdims=True)
        row = jnp.where(lane_row == j, part, row)

    def exchange(stage, partners, row):
        ar_send[stage] = row
        sent = []
        for j, device in enumerate(partners):
            copy = pltpu.make_async_remote_copy(
                src_ref=ar_send.at[stage],
                dst_ref=ar_got.at[stage, j],
                send_sem=ar_send_sem.at[stage, j],
                recv_sem=ar_recv_sem.at[stage, j],
                device_id=device,
                device_id_type=MESH,
            )
            copy.start()
            sent.append(copy)
        return sent

    def gathered(stage, sent, row):
        for copy in sent:
            copy.wait_recv()
        return row + jnp.sum(ar_got[stage], axis=0)

    first = exchange(0, column, row)
    row = gathered(0, first, row)
    second = exchange(1, plane, row)

    for f in range(FIELDS):

        def keep_second(z, i, tile, carry):
            raw[f, z * 8 + i] = tile
            return carry

        complete(2, f, keep_second, 0)

    row = gathered(1, second, row)

    def moved(count):
        return pltpu.roll(jnp.broadcast_to(row, (8, LANES)), LANES - count, 1)

    norm = jnp.where(lane < FIELDS, jnp.broadcast_to(row, (8, LANES)), 1.0)
    beta = moved(3) / norm
    gamma = moved(6) / norm
    delta = moved(9) / norm
    below = beta * delta - gamma * gamma
    below = jnp.where(lane < FIELDS, below, 1.0)
    one_image = (delta - beta * gamma) / below
    two_images = (gamma - beta * beta) / below

    for f in range(FIELDS):
        c = jnp.broadcast_to(one_image[:, f : f + 1], (8, LANES))
        d = jnp.broadcast_to(two_images[:, f : f + 1], (8, LANES))

        def combine(z, carry):
            for i in range(8):
                rhs = full[0, f, z * 8 + i]
                image = full[1, f, z * 8 + i]
                twice = raw[f, z * 8 + i]
                sol[f, z, pl.ds(i, 8, stride=8), :] = c * rhs - d * image
                res[f, z, pl.ds(i, 8, stride=8), :] = rhs - c * image + d * twice
            return carry

        lax.fori_loop(0, 8, combine, 0)

    for copy in first + second:
        copy.wait_send()
    for ph in range(PHASES):
        for f in range(FIELDS):
            finish_sends(ph, f)


def shards(source_terms, diffusion, mass_coefficient):
    shape = source_terms.shape
    field = (FIELDS, TILES, 8, LANES)
    f32 = jnp.float32
    operators = jnp.asarray(lane_operators())
    return pl.pallas_call(
        kernel,
        out_shape=(jax.ShapeDtypeStruct(shape, f32), jax.ShapeDtypeStruct(shape, f32)),
        in_specs=[pl.BlockSpec(memory_space=pltpu.HBM)] * 4,
        out_specs=(
            pl.BlockSpec(memory_space=pltpu.VMEM),
            pl.BlockSpec(memory_space=pltpu.VMEM),
        ),
        scratch_shapes=[
            pltpu.VMEM(shape, f32),
            pltpu.VMEM(shape, f32),
            pltpu.VMEM(mass_coefficient.shape, f32),
            pltpu.VMEM((2, LANES, LANES), f32),
            pltpu.VMEM((2, 2 * LANES, 2 * LANES), jnp.bfloat16),
            pltpu.VMEM(field, f32),
            pltpu.VMEM(field[1:], f32),
            pltpu.VMEM((PHASES,) + field, f32),
            pltpu.VMEM((2,) + field, f32),
            pltpu.VMEM(field, f32),
            pltpu.VMEM((PHASES, FIELDS, 8, LANES), f32),
            pltpu.VMEM((PHASES, FIELDS, 2, 8, 8, LANES), f32),
            pltpu.VMEM((PHASES, FIELDS, 6, 8, LANES), f32),
            pltpu.VMEM((12, 8, LANES), f32),
            pltpu.VMEM((2, 1, LANES), f32),
            pltpu.VMEM((2, 15, 1, LANES), f32),
            pltpu.SemaphoreType.DMA((8,)),
            pltpu.SemaphoreType.DMA((PHASES, FIELDS, 8)),
            pltpu.SemaphoreType.DMA((PHASES, FIELDS, 8)),
            pltpu.SemaphoreType.DMA((2, 15)),
            pltpu.SemaphoreType.DMA((2, 15)),
        ],
        compiler_params=pltpu.CompilerParams(
            collective_id=0, has_side_effects=True, vmem_limit_bytes=40 * 1024 * 1024
        ),
    )(source_terms, diffusion, mass_coefficient, operators)


def solution(mesh):
    in_specs = (
        P(None, "axial", None, "azi"),
        P(None, "axial", None, "azi"),
        P("axial", None, "azi"),
    )
    out_specs = (P(None, "axial", None, "azi"), P(None, "axial", None, "azi"))
    return jax.shard_map(shards, mesh=mesh, in_specs=in_specs, out_specs=out_specs, check_vma=False)
```

time: 342 us -> 56.4 us (0.16); the launches traced: 337 us -> 56.1 us
  blocking collectives: 224 us -> 0 us
  Pallas kernels: 0 us -> 49.6 us
  waiting for transfers between devices: 30 us -> 0 us
  starting transfers between devices: 27 us -> 0 us
  other arithmetic: 21 us -> 0 us
  local copies, waits for them, and re-layouts: 20.8 us -> 5.87 us
  matrix products: 12.3 us -> 0 us
    psum x3 -> x0, blocking collectives: 224 us -> none  [the longest x2 146 us: squares(): lax.psum(jnp.sum(residual * residual * inverse_mult, axis=(1, 2, 3)), ('a...]
    pallas_call x0 -> x1, Pallas kernels: none -> 49.6 us  [shards(): pl.pallas_call(kernel, out_shape=(jax.ShapeDtypeStruct(shape, f32), jax.S...]
    ppermute x12 -> x0, waiting for transfers between devices: 30 us -> none  [the longest x6 21.4 us: with_halo(): before = lax.ppermute(last, axis, up)]
    ppermute x12 -> x0, starting transfers between devices: 27 us -> none  [the longest x6 18.4 us: with_halo(): after = lax.ppermute(leading, axis, down)]
    dot_general x12 -> x0, matrix products: 12.3 us -> none  [the longest x2 3.34 us: shards(): jnp.einsum('zy,fzra->fyra', matrix_z, scaled * grad_z, precision=high)]
    slice x7 -> x0, local copies, waits for them, and re-layouts: 10.1 us -> none  [the longest x5 7.77 us: with_halo(): last = lax.slice_in_dim(value, length - width, length, axis=dim)]
    slice x3 -> x0, other arithmetic: 7.3 us -> none  [with_halo(): last = lax.slice_in_dim(value, length - width, length, axis=dim)]
    ppermute x6 -> x0, local copies, waits for them, and re-layouts: 6.08 us -> none  [the longest x3 3.48 us: with_halo(): after = lax.ppermute(leading, axis, down)]
  transfers between devices with their start and end apart: 12 -> 0, of which waited for: 8 -> 0; matrix products, arithmetic and copies ran while one was open for 2% -> 0% of each run, Pallas kernels for 0% -> 0%
where the time goes in v1:
time: 56.4 us; the launch traced here: 56.1 us
  Pallas kernels  49.6 us (88%)
  local copies, waits for them, and re-layouts  5.87 us (10%)
  between operations  0.65 us (1%)
    pallas_call x1, Pallas kernels, shards(): pl.pallas_call(kernel, out_shape=(jax.ShapeDtypeStruct(shape, f32), jax.S...  49.6 us
    unnamed x10, local copies, waits for them, and re-layouts  5.87 us

profile of v1, /device:TPU:1, one launch (start us, length us, event | category | flops | bytes accessed | tf_op | source)
XLA Modules:
  0.0 56.1 jit_solution(9783951447709924373)
XLA Ops:
  0.6 0.0 copy-start
  0.6 1.1 %copy-done = f32[3,8,64,128]{3,2,1,0:T(8,128)S(1)} copy-done((f32[3,8,64,128]{3,2,1,0:T(8,128)S(1)}, f32[3,8,64,128]{3,2,1,0:T(8,128)}, u32[]{:S(2)}) %copy-start) | copy-done | bytes 786456
  1.8 0.0 copy-start.1
  1.8 1.1 %copy-done.1 = f32[3,8,64,128]{3,2,1,0:T(8,128)S(1)} copy-done((f32[3,8,64,128]{3,2,1,0:T(8,128)S(1)}, f32[3,8,64,128]{3,2,1,0:T(8,128)}, u32[]{:S(2)}) %copy-start.1) | copy-done | bytes 786456
  2.9 0.0 copy-start.2
  2.9 0.9 %copy-done.2 = f32[8,64,128]{2,1,0:T(8,128)S(1)} copy-done((f32[8,64,128]{2,1,0:T(8,128)S(1)}, f32[8,64,128]{2,1,0:T(8,128)}, u32[]{:S(2)}) %copy-start.2) | copy-done | bytes 262168
  3.8 0.0 copy-start.3
  3.9 0.9 %copy-done.3 = f32[2,128,128]{2,1,0:T(8,128)S(1)} copy-done((f32[2,128,128]{2,1,0:T(8,128)S(1)}, f32[2,128,128]{2,1,0:T(8,128)}, u32[]{:S(2)}) %copy-start.3) | copy-done | bytes 131096
  4.8 49.6 %shard_map.59 = (f32[3,8,64,128]{3,2,1,0:T(8,128)S(1)}, f32[3,8,64,128]{3,2,1,0:T(8,128)S(1)}) custom-call(f32[3,8,64,128]{3,2,1,0:T(8,128)S(1)} %copy-done, f32[3,8,64,128]{3,2,1,0:T(8,128)S(1)} %copy-done.1, f32[8,64,128]{2,1,0:T(8,128)S(1)} %copy-done.2, f32[2,128,128]{2,1,0:T(8,128)S(1)} %copy-done.3), custom_call_target="tpu_custom_call" | custom-call | tf_op jit(solution)/shard_map/pallas_call | solution.py:492
  54.4 0.9 %copy.8 = f32[3,8,64,128]{3,2,1,0:T(8,128)} copy(f32[3,8,64,128]{3,2,1,0:T(8,128)S(1)} %get-tuple-element.4) | data formatting | bytes 1572864
  55.3 0.9 %copy.9 = f32[3,8,64,128]{3,2,1,0:T(8,128)} copy(f32[3,8,64,128]{3,2,1,0:T(8,128)S(1)} %get-tuple-element.5) | data formatting | bytes 1572864
Async XLA Ops:
  0.6 1.1 %copy-start = (f32[3,8,64,128]{3,2,1,0:T(8,128)S(1)}, f32[3,8,64,128]{3,2,1,0:T(8,128)}, u32[]{:S(2)}) copy-start(f32[3,8,64,128]{3,2,1,0:T(8,128)} %src_hbm.1) | copy-start | bytes 2359300
  1.8 1.1 %copy-start.1 = (f32[3,8,64,128]{3,2,1,0:T(8,128)S(1)}, f32[3,8,64,128]{3,2,1,0:T(8,128)}, u32[]{:S(2)}) copy-start(f32[3,8,64,128]{3,2,1,0:T(8,128)} %dif_hbm.1) | copy-start | bytes 2359300
  2.9 0.9 %copy-start.2 = (f32[8,64,128]{2,1,0:T(8,128)S(1)}, f32[8,64,128]{2,1,0:T(8,128)}, u32[]{:S(2)}) copy-start(f32[8,64,128]{2,1,0:T(8,128)} %mas_hbm.1) | copy-start | bytes 786436
  3.8 0.9 %copy-start.3 = (f32[2,128,128]{2,1,0:T(8,128)S(1)}, f32[2,128,128]{2,1,0:T(8,128)}, u32[]{:S(2)}) copy-start(f32[2,128,128]{2,1,0:T(8,128)} %constant.2.clone.wts_hbm) | copy-start | bytes 393220

commit v2 on v1

--- a/solution.py
+++ b/solution.py
@@ -207,7 +207,7 @@
             own[ph, f, z * 8 + i] = tile
             turned = pltpu.roll(tile, 2 * i, 1) if i else tile
             line = jnp.where(pair_of_lane == i, turned, line)
-        return jnp.where(group_of_lane == z, pltpu.roll(line, z * 16, 1), faces)
+        return jnp.where(group_of_lane == z, pltpu.roll(line, z * 16, 1) if z else line, faces)
 
     def copies(ph, f):
         def remote(source, target, slot, device):
@@ -299,7 +299,7 @@
         faces = faces + jnp.where(group_of_lane == 7, high, 0.0)
 
         def one(z, carry, plane):
-            line = pltpu.roll(faces, lax.rem(LANES - z * 16, LANES), 1)
+            line = pltpu.roll(faces, LANES - z * 16, 1) if z else faces
             for i in range(8):
                 turned = pltpu.roll(line, LANES - 2 * i, 1) if i else line
                 tile = own[ph, f, z * 8 + i] + jnp.where(outer, turned, 0.0)
@@ -309,7 +309,8 @@
             return carry
 
         carry = one(0, carry, 0)
-        carry = lax.fori_loop(1, 7, lambda z, c: one(z, c, None), carry)
+        for z in range(1, 7):
+            carry = one(z, carry, None)
         return one(7, carry, 1)
 
     def split_dot(values, which):
@@ -334,7 +335,8 @@
                 raw[f, z * 8 + i] = raw[f, z * 8 + i] + (back[z] + massive[z * 8 + i] * tiles[z])
             return carry
 
-        lax.fori_loop(0, 8, along_axial, 0)
+        for i in range(8):
+            along_axial(i, 0)
 
         def along_radius(z, carry):
             total, faces = carry
@@ -348,7 +350,9 @@
                 raw[f, z * 8 + i] = back[i]
             return total, assemble_own(k + 1, f, z, back, faces)
 
-        total, faces = lax.fori_loop(0, 8, along_radius, (zeros, zeros))
+        total, faces = zeros, zeros
+        for z in range(8):
+            total, faces = along_radius(z, (total, faces))
         packed[k + 1, f] = faces
         return total
 
@@ -361,7 +365,10 @@
         def gather(z, faces):
             return assemble_own(0, f, z, [native(src, f, z, i) for i in range(8)], faces)
 
-        packed[0, f] = lax.fori_loop(0, 8, gather, zeros)
+        faces = zeros
+        for z in range(8):
+            faces = gather(z, faces)
+        packed[0, f] = faces
 
     around = axial * 0 + 2 + 30 + jnp.where(has_low, 3, 0) + jnp.where(has_high, 3, 0)
     pl.semaphore_wait(barrier, around)
@@ -475,7 +482,8 @@
                 res[f, z, pl.ds(i, 8, stride=8), :] = rhs - c * image + d * twice
             return carry
 
-        lax.fori_loop(0, 8, combine, 0)
+        for z in range(8):
+            combine(z, 0)
 
     for copy in first + second:
         copy.wait_send()
@@ -523,7 +531,7 @@
         compiler_params=pltpu.CompilerParams(
             collective_id=0, has_side_effects=True, vmem_limit_bytes=40 * 1024 * 1024
         ),
-    )(source_terms, diffusion, mass_coefficient, operators)
+    )(*(pltpu.with_memory_space_constraint(x, pltpu.HBM) for x in (source_terms, diffusion, mass_coefficient, operators)))
 
 
 def solution(mesh):

time: 56.4 us -> 37.6 us (0.67)
  Pallas kernels: 49.6 us -> 35.1 us
  local copies, waits for them, and re-layouts: 5.87 us -> 1.76 us
    pallas_call x1, Pallas kernels: 49.6 us -> 35.1 us  [shards(): pl.pallas_call(kernel, out_shape=(jax.ShapeDtypeStruct(shape, f32), jax.S...]
    unnamed x10 -> x2, local copies, waits for them, and re-layouts: 5.87 us -> 1.76 us
where the time goes in v2:
time: 37.6 us; the launch traced here: 37.5 us
  Pallas kernels  35.1 us (93%)
  local copies, waits for them, and re-layouts  1.76 us (5%)
  between operations  0.64 us (2%)
    pallas_call x1, Pallas kernels, shards(): pl.pallas_call(kernel, out_shape=(jax.ShapeDtypeStruct(shape, f32), jax.S...  35.1 us
    unnamed x2, local copies, waits for them, and re-layouts  1.76 us

profile of v2, /device:TPU:1, one launch (start us, length us, event | category | flops | bytes accessed | tf_op | source)
XLA Modules:
  0.0 37.5 jit_solution(347633686829557102)
XLA Ops:
  0.6 35.1 %shard_map.59 = (f32[3,8,64,128]{3,2,1,0:T(8,128)S(1)}, f32[3,8,64,128]{3,2,1,0:T(8,128)S(1)}) custom-call(f32[3,8,64,128]{3,2,1,0:T(8,128)} %src_hbm.1, f32[3,8,64,128]{3,2,1,0:T(8,128)} %dif_hbm.1, f32[8,64,128]{2,1,0:T(8,128)} %mas_hbm.1, f32[2,128,128]{2,1,0:T(8,128)} %constant.2.clone.wts_hbm), custom_call_target="tpu_custom_call" | custom-call | tf_op jit(solution)/shard_map/pallas_call | solution.py:500
  35.7 0.9 %copy.8 = f32[3,8,64,128]{3,2,1,0:T(8,128)} copy(f32[3,8,64,128]{3,2,1,0:T(8,128)S(1)} %get-tuple-element.4) | data formatting | bytes 1572864
  36.6 0.9 %copy.9 = f32[3,8,64,128]{3,2,1,0:T(8,128)} copy(f32[3,8,64,128]{3,2,1,0:T(8,128)S(1)} %get-tuple-element.5) | data formatting | bytes 1572864

commit v3 on v2

--- a/solution.py
+++ b/solution.py
@@ -9,6 +9,7 @@
 MESH = pl.DeviceIdType.MESH
 FIELDS = 3
 PHASES = 3
+PIECES = 1
 LANES = 128
 TILES = 64
 
@@ -97,8 +98,10 @@
     dif_hbm,
     mas_hbm,
     wts_hbm,
-    sol,
-    res,
+    rhs_out,
+    image_out,
+    twice_out,
+    coef_out,
     src,
     dif,
     mas,
@@ -400,6 +403,7 @@
 
         def keep_rhs(z, i, tile, total):
             full[0, f, z * 8 + i] = tile
+            rhs_out[f, z, pl.ds(i, 8, stride=8), :] = tile
             return total + tile * native(src, f, z, i)
 
         dots[f] = complete(0, f, keep_rhs, zeros)
@@ -410,6 +414,7 @@
 
         def keep_image(z, i, tile, total):
             full[1, f, z * 8 + i] = tile
+            image_out[f, z, pl.ds(i, 8, stride=8), :] = tile
             return total + tile * raw[f, z * 8 + i]
 
         dots[6 + f] = complete(1, f, keep_image, zeros)
@@ -450,7 +455,7 @@
     for f in range(FIELDS):
 
         def keep_second(z, i, tile, carry):
-            raw[f, z * 8 + i] = tile
+            twice_out[f, z, pl.ds(i, 8, stride=8), :] = tile
             return carry
 
         complete(2, f, keep_second, 0)
@@ -469,21 +474,8 @@
     one_image = (delta - beta * gamma) / below
     two_images = (gamma - beta * beta) / below
 
-    for f in range(FIELDS):
-        c = jnp.broadcast_to(one_image[:, f : f + 1], (8, LANES))
-        d = jnp.broadcast_to(two_images[:, f : f + 1], (8, LANES))
-
-        def combine(z, carry):
-            for i in range(8):
-                rhs = full[0, f, z * 8 + i]
-                image = full[1, f, z * 8 + i]
-                twice = raw[f, z * 8 + i]
-                sol[f, z, pl.ds(i, 8, stride=8), :] = c * rhs - d * image
-                res[f, z, pl.ds(i, 8, stride=8), :] = rhs - c * image + d * twice
-            return carry
-
-        for z in range(8):
-            combine(z, 0)
+    coef_out[0] = one_image
+    coef_out[1] = two_images
 
     for copy in first + second:
         copy.wait_send()
@@ -492,19 +484,42 @@
             finish_sends(ph, f)
 
 
+def combine(rhs, image, twice, coefs, sol_hbm, res_hbm, sol, res, sems):
+    rows = 8 // PIECES
+    copies = []
+    for f in range(FIELDS):
+        c = jnp.broadcast_to(coefs[0][:, f : f + 1], (8, LANES))
+        d = jnp.broadcast_to(coefs[1][:, f : f + 1], (8, LANES))
+        for piece in range(PIECES):
+            part = pl.ds(piece * rows, rows)
+            for z in range(piece * rows, (piece + 1) * rows):
+                for e in range(8):
+                    at = (f, z, pl.ds(e * 8, 8))
+                    first = image[at]
+                    sol[at] = c * rhs[at] - d * first
+                    res[at] = rhs[at] - c * first + d * twice[at]
+            for k, (vmem, hbm) in enumerate(((sol, sol_hbm), (res, res_hbm))):
+                copy = pltpu.make_async_copy(
+                    vmem.at[f, part], hbm.at[f, part], sems.at[k, f, piece]
+                )
+                copy.start()
+                copies.append(copy)
+    for copy in copies:
+        copy.wait()
+
+
 def shards(source_terms, diffusion, mass_coefficient):
     shape = source_terms.shape
     field = (FIELDS, TILES, 8, LANES)
     f32 = jnp.float32
     operators = jnp.asarray(lane_operators())
-    return pl.pallas_call(
+    rhs, image, twice, coefs = pl.pallas_call(
         kernel,
-        out_shape=(jax.ShapeDtypeStruct(shape, f32), jax.ShapeDtypeStruct(shape, f32)),
+        out_shape=tuple(
+            jax.ShapeDtypeStruct(s, f32) for s in (shape, shape, shape, (2, 8, LANES))
+        ),
         in_specs=[pl.BlockSpec(memory_space=pltpu.HBM)] * 4,
-        out_specs=(
-            pl.BlockSpec(memory_space=pltpu.VMEM),
-            pl.BlockSpec(memory_space=pltpu.VMEM),
-        ),
+        out_specs=(pl.BlockSpec(memory_space=pltpu.VMEM),) * 4,
         scratch_shapes=[
             pltpu.VMEM(shape, f32),
             pltpu.VMEM(shape, f32),
@@ -532,6 +547,17 @@
             collective_id=0, has_side_effects=True, vmem_limit_bytes=40 * 1024 * 1024
         ),
     )(*(pltpu.with_memory_space_constraint(x, pltpu.HBM) for x in (source_terms, diffusion, mass_coefficient, operators)))
+    return pl.pallas_call(
+        combine,
+        out_shape=(jax.ShapeDtypeStruct(shape, f32),) * 2,
+        in_specs=[pl.BlockSpec(memory_space=pltpu.VMEM)] * 4,
+        out_specs=(pl.BlockSpec(memory_space=pltpu.HBM),) * 2,
+        scratch_shapes=[
+            pltpu.VMEM(shape, f32),
+            pltpu.VMEM(shape, f32),
+            pltpu.SemaphoreType.DMA((2, FIELDS, PIECES)),
+        ],
+    )(*(pltpu.with_memory_space_constraint(x, pltpu.VMEM) for x in (rhs, image, twice, coefs)))
 
 
 def solution(mesh):

time: 37.6 us -> 36.8 us (0.979)
  local copies, waits for them, and re-layouts: 1.76 us -> 0 us
  Pallas kernels: 35.1 us -> 36.1 us
    unnamed x2 -> x0, local copies, waits for them, and re-layouts: 1.76 us -> none
    pallas_call x1 -> x2, Pallas kernels: 35.1 us -> 36.1 us  [the longest x1 34.8 us: shards(): pl.pallas_call(kernel, out_shape=tuple((jax.ShapeDtypeStruct(s, f32) for...]
where the time goes in v3:
time: 36.8 us; the launch traced here: 36.7 us
  Pallas kernels  36.1 us (98%)
  between operations  0.64 us (2%)
    pallas_call x1, Pallas kernels, shards(): pl.pallas_call(kernel, out_shape=tuple((jax.ShapeDtypeStruct(s, f32) for...  34.8 us
    pallas_call x1, Pallas kernels, shards(): pl.pallas_call(combine, out_shape=(jax.ShapeDtypeStruct(shape, f32),) * 2...  1.32 us

profile of v3, /device:TPU:1, one launch (start us, length us, event | category | flops | bytes accessed | tf_op | source)
XLA Modules:
  0.0 36.7 jit_solution(3798790330146453598)
XLA Ops:
  0.6 34.8 %shard_map.59 = (f32[3,8,64,128]{3,2,1,0:T(8,128)S(1)}, f32[3,8,64,128]{3,2,1,0:T(8,128)S(1)}, f32[3,8,64,128]{3,2,1,0:T(8,128)S(1)}, f32[2,8,128]{2,1,0:T(8,128)S(1)}) custom-call(f32[3,8,64,128]{3,2,1,0:T(8,128)} %src_hbm.1, f32[3,8,64,128]{3,2,1,0:T(8,128)} %dif_hbm.1, f32[8,64,128]{2,1,0:T(8,128)} %mas_hbm.1, f32[2,128,128]{2,1,0:T(8,128)} %constant.2.clone.wts_hbm), custom_call_target="tpu_custom_call" | custom-call | tf_op jit(solution)/shard_map/pallas_call | solution.py:516
  35.4 1.3 %shard_map.60 = (f32[3,8,64,128]{3,2,1,0:T(8,128)}, f32[3,8,64,128]{3,2,1,0:T(8,128)}) custom-call(f32[3,8,64,128]{3,2,1,0:T(8,128)S(1)} %get-tuple-element.6.rhs, f32[3,8,64,128]{3,2,1,0:T(8,128)S(1)} %get-tuple-element.7.image, f32[3,8,64,128]{3,2,1,0:T(8,128)S(1)} %get-tuple-element.8.twice, f32[2,8,128]{2,1,0:T(8,128)S(1)} %get-tuple-element.9.coefs), custom_call_target="tpu_custom_call" | custom-call | tf_op jit(solution)/shard_map/pallas_call | solution.py:550

commit v4 on v3

--- a/solution.py
+++ b/solution.py
@@ -403,7 +403,6 @@
 
         def keep_rhs(z, i, tile, total):
             full[0, f, z * 8 + i] = tile
-            rhs_out[f, z, pl.ds(i, 8, stride=8), :] = tile
             return total + tile * native(src, f, z, i)
 
         dots[f] = complete(0, f, keep_rhs, zeros)
@@ -414,7 +413,6 @@
 
         def keep_image(z, i, tile, total):
             full[1, f, z * 8 + i] = tile
-            image_out[f, z, pl.ds(i, 8, stride=8), :] = tile
             return total + tile * raw[f, z * 8 + i]
 
         dots[6 + f] = complete(1, f, keep_image, zeros)
@@ -451,6 +449,11 @@
     first = exchange(0, column, row)
     row = gathered(0, first, row)
     second = exchange(1, plane, row)
+    for f in range(FIELDS):
+        for z in range(8):
+            for i in range(8):
+                rhs_out[f, z, pl.ds(i, 8, stride=8), :] = full[0, f, z * 8 + i]
+                image_out[f, z, pl.ds(i, 8, stride=8), :] = full[1, f, z * 8 + i]
 
     for f in range(FIELDS):
 
@@ -460,6 +463,11 @@
 
         complete(2, f, keep_second, 0)
 
+    for copy in first + second:
+        copy.wait_send()
+    for ph in range(PHASES):
+        for f in range(FIELDS):
+            finish_sends(ph, f)
     row = gathered(1, second, row)
 
     def moved(count):
@@ -476,12 +484,6 @@
 
     coef_out[0] = one_image
     coef_out[1] = two_images
-
-    for copy in first + second:
-        copy.wait_send()
-    for ph in range(PHASES):
-        for f in range(FIELDS):
-            finish_sends(ph, f)
 
 
 def combine(rhs, image, twice, coefs, sol_hbm, res_hbm, sol, res, sems):

time: 36.8 us -> 36.6 us (level)
  no operation moved by 1% of the time
where the time goes in v4:
time: 36.6 us; the launch traced here: 36.5 us
  Pallas kernels  35.9 us (98%)
  between operations  0.64 us (2%)
    pallas_call x1, Pallas kernels, shards(): pl.pallas_call(kernel, out_shape=tuple((jax.ShapeDtypeStruct(s, f32) for...  34.6 us
    pallas_call x1, Pallas kernels, shards(): pl.pallas_call(combine, out_shape=(jax.ShapeDtypeStruct(shape, f32),) * 2...  1.32 us

profile of v4, /device:TPU:1, one launch (start us, length us, event | category | flops | bytes accessed | tf_op | source)
XLA Modules:
  0.0 36.5 jit_solution(9567986964822659795)
XLA Ops:
  0.6 34.6 %shard_map.59 = (f32[3,8,64,128]{3,2,1,0:T(8,128)S(1)}, f32[3,8,64,128]{3,2,1,0:T(8,128)S(1)}, f32[3,8,64,128]{3,2,1,0:T(8,128)S(1)}, f32[2,8,128]{2,1,0:T(8,128)S(1)}) custom-call(f32[3,8,64,128]{3,2,1,0:T(8,128)} %src_hbm.1, f32[3,8,64,128]{3,2,1,0:T(8,128)} %dif_hbm.1, f32[8,64,128]{2,1,0:T(8,128)} %mas_hbm.1, f32[2,128,128]{2,1,0:T(8,128)} %constant.2.clone.wts_hbm), custom_call_target="tpu_custom_call" | custom-call | tf_op jit(solution)/shard_map/pallas_call | solution.py:518
  35.2 1.3 %shard_map.60 = (f32[3,8,64,128]{3,2,1,0:T(8,128)}, f32[3,8,64,128]{3,2,1,0:T(8,128)}) custom-call(f32[3,8,64,128]{3,2,1,0:T(8,128)S(1)} %get-tuple-element.6.rhs, f32[3,8,64,128]{3,2,1,0:T(8,128)S(1)} %get-tuple-element.7.image, f32[3,8,64,128]{3,2,1,0:T(8,128)S(1)} %get-tuple-element.8.twice, f32[2,8,128]{2,1,0:T(8,128)S(1)} %get-tuple-element.9.coefs), custom_call_target="tpu_custom_call" | custom-call | tf_op jit(solution)/shard_map/pallas_call | solution.py:552

commit v5 on v4

--- a/solution.py
+++ b/solution.py
@@ -327,7 +327,7 @@
     def operate(k, f):
         values = full[k, f].reshape(TILES * 8, LANES)
         gradient = split_dot(values, 0) * scaled[f].reshape(TILES * 8, LANES)
-        raw[f] = split_dot(gradient, 1).reshape(TILES, 8, LANES)
+        raw[k, f] = split_dot(gradient, 1).reshape(TILES, 8, LANES)
 
         def along_axial(i, carry):
             tiles = [full[k, f, z * 8 + i] for z in range(8)]
@@ -335,7 +335,7 @@
             gradient = [scaled[f, z * 8 + i] * gradient[z] for z in range(8)]
             back = mix(DERIVATIVE.T, gradient)
             for z in range(8):
-                raw[f, z * 8 + i] = raw[f, z * 8 + i] + (back[z] + massive[z * 8 + i] * tiles[z])
+                raw[k, f, z * 8 + i] = raw[k, f, z * 8 + i] + (back[z] + massive[z * 8 + i] * tiles[z])
             return carry
 
         for i in range(8):
@@ -347,10 +347,12 @@
             gradient = mix(DERIVATIVE, tiles)
             gradient = [scaled[f, z * 8 + i] * gradient[i] for i in range(8)]
             back = mix(DERIVATIVE.T, gradient)
-            back = [raw[f, z * 8 + i] + back[i] for i in range(8)]
+            back = [raw[k, f, z * 8 + i] + back[i] for i in range(8)]
             for i in range(8):
-                total = total + tiles[i] * back[i]
-                raw[f, z * 8 + i] = back[i]
+                if k:
+                    total = total + tiles[i] * back[i]
+                else:
+                    raw[k, f, z * 8 + i] = back[i]
             return total, assemble_own(k + 1, f, z, back, faces)
 
         total, faces = zeros, zeros
@@ -403,27 +405,41 @@
 
         def keep_rhs(z, i, tile, total):
             full[0, f, z * 8 + i] = tile
-            return total + tile * native(src, f, z, i)
-
-        dots[f] = complete(0, f, keep_rhs, zeros)
-        dots[3 + f] = operate(0, f)
+            return total
+
+        complete(0, f, keep_rhs, 0)
+        operate(0, f)
         send(1, f)
+
+    lane_row = lax.broadcasted_iota(jnp.int32, (1, LANES), 1)
+
+    def add_to_row(row, j, total):
+        part = jnp.sum(jnp.sum(total, axis=0, keepdims=True), axis=1, keepdims=True)
+        return jnp.where(lane_row == j, part, row)
+
+    row = jnp.zeros((1, LANES), jnp.float32)
+    for f in range(FIELDS):
+        alpha, beta = zeros, zeros
+        for z in range(8):
+            for i in range(8):
+                tile = full[0, f, z * 8 + i]
+                alpha = alpha + tile * native(src, f, z, i)
+                beta = beta + tile * raw[0, f, z * 8 + i]
+        row = add_to_row(row, f, alpha)
+        row = add_to_row(row, 3 + f, beta)
 
     for f in range(FIELDS):
 
         def keep_image(z, i, tile, total):
             full[1, f, z * 8 + i] = tile
-            return total + tile * raw[f, z * 8 + i]
+            return total + tile * raw[0, f, z * 8 + i]
 
         dots[6 + f] = complete(1, f, keep_image, zeros)
         dots[9 + f] = operate(1, f)
         send(2, f)
 
-    lane_row = lax.broadcasted_iota(jnp.int32, (1, LANES), 1)
-    row = jnp.zeros((1, LANES), jnp.float32)
-    for j in range(12):
-        part = jnp.sum(jnp.sum(dots[j], axis=0, keepdims=True), axis=1, keepdims=True)
-        row = jnp.where(lane_row == j, part, row)
+    for j in range(6, 12):
+        row = add_to_row(row, j, dots[j])
 
     def exchange(stage, partners, row):
         ar_send[stage] = row
@@ -532,7 +548,7 @@
             pltpu.VMEM(field[1:], f32),
             pltpu.VMEM((PHASES,) + field, f32),
             pltpu.VMEM((2,) + field, f32),
-            pltpu.VMEM(field, f32),
+            pltpu.VMEM((2,) + field, f32),
             pltpu.VMEM((PHASES, FIELDS, 8, LANES), f32),
             pltpu.VMEM((PHASES, FIELDS, 2, 8, 8, LANES), f32),
             pltpu.VMEM((PHASES, FIELDS, 6, 8, LANES), f32),

time: 36.6 us -> 36.6 us (level)
  no operation moved by 1% of the time
where the time goes in v5:
time: 36.6 us; the launch traced here: 36.5 us
  Pallas kernels  35.9 us (98%)
  between operations  0.64 us (2%)
    pallas_call x1, Pallas kernels, shards(): pl.pallas_call(kernel, out_shape=tuple((jax.ShapeDtypeStruct(s, f32) for...  34.6 us
    pallas_call x1, Pallas kernels, shards(): pl.pallas_call(combine, out_shape=(jax.ShapeDtypeStruct(shape, f32),) * 2...  1.32 us

profile of v5, /device:TPU:1, one launch (start us, length us, event | category | flops | bytes accessed | tf_op | source)
XLA Modules:
  0.0 36.5 jit_solution(10245458993155322251)
XLA Ops:
  0.6 34.6 %shard_map.59 = (f32[3,8,64,128]{3,2,1,0:T(8,128)S(1)}, f32[3,8,64,128]{3,2,1,0:T(8,128)S(1)}, f32[3,8,64,128]{3,2,1,0:T(8,128)S(1)}, f32[2,8,128]{2,1,0:T(8,128)S(1)}) custom-call(f32[3,8,64,128]{3,2,1,0:T(8,128)} %src_hbm.1, f32[3,8,64,128]{3,2,1,0:T(8,128)} %dif_hbm.1, f32[8,64,128]{2,1,0:T(8,128)} %mas_hbm.1, f32[2,128,128]{2,1,0:T(8,128)} %constant.2.clone.wts_hbm), custom_call_target="tpu_custom_call" | custom-call | tf_op jit(solution)/shard_map/pallas_call | solution.py:534
  35.2 1.3 %shard_map.60 = (f32[3,8,64,128]{3,2,1,0:T(8,128)}, f32[3,8,64,128]{3,2,1,0:T(8,128)}) custom-call(f32[3,8,64,128]{3,2,1,0:T(8,128)S(1)} %get-tuple-element.6.rhs, f32[3,8,64,128]{3,2,1,0:T(8,128)S(1)} %get-tuple-element.7.image, f32[3,8,64,128]{3,2,1,0:T(8,128)S(1)} %get-tuple-element.8.twice, f32[2,8,128]{2,1,0:T(8,128)S(1)} %get-tuple-element.9.coefs), custom_call_target="tpu_custom_call" | custom-call | tf_op jit(solution)/shard_map/pallas_call | solution.py:568
